TPU v7x, 256 devices: a whole 4x4x8 slice. The times are simulated.
256 devices in a mesh: ctx: 32 (over x, z), tp: 4 (over y_hi, core), grp: 2 (over y_lo).
Axes of the slice: x: 4, y: 4 (y_hi: 2, y_lo: 2; y = y_hi * 2 + y_lo), z: 8, core: 2. Of those that a mesh axis runs over, the one named last changes fastest.
Arguments:
- prefill_query: bfloat16 [4096, 24576], P('ctx', ('tp', 'grp')), may hold values from -80 to 80
- prompt_cache: bfloat16 [4096, 576], P('ctx'), may hold values from -6 to 6
- key_up: bfloat16 [512, 16384], P(None, ('tp', 'grp')), may hold values from -0.5 to 0.5
- value_up: bfloat16 [512, 16384], P(None, ('tp', 'grp')), may hold values from -0.25 to 0.25
- block_place: int32 [64], replicated, may hold values from 0 to 63, each once
- decode_query: bfloat16 [256, 24576], P('ctx', ('tp', 'grp')), may hold values from -80 to 80
- decode_cache: bfloat16 [256, 576], P('ctx'), may hold values from -6 to 6
- row_length: int32 [256], replicated, may hold values from 1 to 4096, as said below
- row_slot: int32 [256], replicated, may hold values from 0 to 255, each once
Outputs:
- prefill_out: bfloat16 [4096, 16384], P(('ctx', 'tp', 'grp'))
- decode_out: bfloat16 [256, 16384], P('ctx', ('tp', 'grp'))
Inputs may be any that keep to these rules, and one draw needn't show every extreme that they name: `row_length`: some row reads the whole prompt. `block_place`: a permutation. `row_slot`: a permutation; slot s belongs to index s // 8 of ctx.
All inputs are finite; a program needn't handle non-finite values.
Results may differ from a plain program's by a relative error of at most 0.027.
Values may be sent and summed in bfloat16 or wider, within the bound.
A program may use at most 128 MiB of HBM per device.

v0:
```python
import functools
import math

import jax
import jax.numpy as jnp
from jax import lax
from jax.experimental import pallas as pl
from jax.experimental.pallas import tpu as pltpu
from jax.sharding import PartitionSpec as P

DL = 512
DR = 64
DN = 128
DV = 128
HD = DN + DR
WIDE = DL + 2 * DR
SPAN = 64
FACTOR = HD**-0.5 * math.log2(math.e)
MASKED = -1e30
NX, NZ = 4, 8
LINE = NX * SPAN
MESH = pl.DeviceIdType.MESH
F32 = jnp.float32
BF16 = jnp.bfloat16


def dot(a, b, ca, cb):
    return lax.dot_general(a, b, (((ca,), (cb,)), ((), ())), preferred_element_type=F32)


def kernel(
    place, length, slots, cache_ref, dq_ref, dc_ref, q_hbm, kup_hbm, vup_hbm, out_ref, dec_ref,
    q_ref, keys, kup, vup, queries, score, top, acc, part_den, base, bias,
    staged, xrows, zsend, zrecv,
    load_sem, send, recv, out_send, out_recv, dec_send, dec_recv,
):
    toks = q_ref.shape[0]
    rows = dq_ref.shape[0]
    heads = q_ref.shape[1] // HD
    count = keys.shape[0]
    pre = heads * toks
    dec = heads * rows
    ctx = lax.axis_index("ctx")
    tp = lax.axis_index("tp")
    grp = lax.axis_index("grp")
    x, z = ctx // NZ, lax.rem(ctx, NZ)
    core = lax.rem(tp, 2)
    member = tp * 2 + grp
    y = tp // 2 * 2 + grp

    def at_x(d):
        return lax.rem(x + d + NX, NX)

    def at_z(d):
        return lax.rem(z + d + NZ, NZ)

    def x_peer(d):
        return (at_x(d) * NZ + z, tp, grp)

    def z_peer(d):
        return (x * NZ + at_z(d), tp, grp)

    def group_peer(d):
        other = lax.rem(member + d, 8)
        return (ctx, other // 2, lax.rem(other, 2))

    def y_peer(d):
        other = lax.rem(y + d, 4)
        return (ctx, other // 2 * 2 + core, lax.rem(other, 2))

    sibling = (ctx, tp + 1 - 2 * core, grp)

    loads = [
        pltpu.make_async_copy(src, dst, load_sem.at[i])
        for i, (src, dst) in enumerate([(q_hbm, q_ref), (kup_hbm, kup), (vup_hbm, vup)])
    ]
    for load in loads:
        load.start()

    barrier = pltpu.get_barrier_semaphore()
    peers = [x_peer(d) for d in range(1, NX)] + [z_peer(d) for d in range(1, NZ)]
    peers += [group_peer(d) for d in range(1, 8)]
    for peer in peers:
        pl.semaphore_signal(barrier, inc=1, device_id=peer, device_id_type=MESH)

    def place_of(half, xx, zz):
        return (zz * 2 + half) * LINE + xx * SPAN

    turned = cache_ref[...].astype(F32).T
    mine = jnp.where(core == 0, turned[:SPAN], turned[SPAN:]).astype(BF16)

    here = pl.ds(pl.multiple_of(place_of(core, x, z), SPAN), SPAN)
    keys[here, : DL + DR] = mine
    keys[here, DL + DR :] = mine[:, DL:]
    pl.semaphore_wait(barrier, len(peers))

    def copy(first, size, sem, peer):
        part = keys.at[pl.ds(pl.multiple_of(first, SPAN), size), :]
        return pltpu.make_async_remote_copy(
            src_ref=part, dst_ref=part, send_sem=send.at[0], recv_sem=recv.at[sem],
            device_id=peer, device_id_type=MESH,
        )

    def landed(sem, size):
        copy(0, size, sem, sibling).wait_recv()

    def start(copies):
        for one in copies:
            one.start()

    def on(which):
        return pl.when(core == which)

    EVEN_Z, ODD_Z, TWIN, EVEN_X, ODD_Y, ODD_X = 0, 5, 10, 15, 20, 25
    far = NZ // 2

    def signs(k):
        return (k,) if k in (0, far) else (k, -k)

    def even_z(k):
        first = place_of(0, x, z)
        start([copy(first, SPAN, EVEN_Z + k, z_peer(dz)) for dz in signs(k)])

    def odd_z(k):
        first = place_of(1, y, z)
        start([copy(first, SPAN, ODD_Z + k, z_peer(dz)) for dz in signs(k)])

    def even_step(k):
        if k:
            landed(EVEN_Z + k, SPAN * len(signs(k)))
        for dz in signs(k):
            start([copy(place_of(0, x, at_z(dz)), SPAN, EVEN_X + k, x_peer(d)) for d in (1, 3, 2)])

    def odd_step(k):
        landed(ODD_Z + k, SPAN * len(signs(k)))
        for dz in signs(k):
            start([copy(place_of(1, y, at_z(dz)), SPAN, ODD_Y + k, y_peer(d)) for d in (1, 3, 2)])

    def twin(dz):
        return copy(place_of(core, 0, at_z(dz)), LINE, TWIN + abs(dz), sibling)

    def even_line(k):
        landed(EVEN_X + k, 3 * SPAN * len(signs(k)))
        start([twin(dz) for dz in signs(k)])

    def odd_line(k):
        landed(ODD_Y + k if k else ODD_X, 3 * SPAN * len(signs(k)))
        start([twin(dz) for dz in signs(k)])

    def twins_landed(k):
        landed(TWIN + k, LINE * len(signs(k)))

    @on(0)
    def _():
        even_z(1)

    @on(1)
    def _():
        start([copy(place_of(1, x, z), SPAN, ODD_X, x_peer(d)) for d in (1, 3, 2)])

    @pl.when((core == 1) & (x == y))
    def _():
        odd_z(1)

    loads[0].wait()
    loads[1].wait()

    def absorb(pair):
        at = pl.ds(pl.multiple_of(pair * 2 * HD, 2 * HD), 2 * HD)
        both = q_ref[:, at].astype(F32)
        dboth = dq_ref[:, at].astype(F32)
        kept = []
        for sub in range(2):
            h = pair * 2 + sub
            every = jnp.concatenate([both, dboth, dboth], axis=0)[:, sub * HD : (sub + 1) * HD]
            block = kup[:, pl.ds(pl.multiple_of(h * DN, DN), DN)]
            absorbed = (dot(every[:, :DN].astype(BF16), block, 1, 1) * FACTOR).astype(BF16)
            rope = every[:, DN:] * FACTOR
            high = rope.astype(BF16).astype(F32)
            rope = jnp.concatenate([high, rope - high], axis=1).astype(BF16)
            here = pl.ds(pl.multiple_of(h * toks, toks), toks)
            queries[here, :DL] = absorbed[:toks]
            queries[here, DL:] = rope[:toks]
            kept.append((absorbed[toks:].astype(F32)[:rows], rope[toks:].astype(F32)[:rows]))
        here = pl.ds(pl.multiple_of(pre + pair * 2 * rows, 2 * rows), 2 * rows)
        queries[here, :DL] = jnp.concatenate([kept[0][0], kept[1][0]], axis=0).astype(BF16)
        queries[here, DL:] = jnp.concatenate([kept[0][1], kept[1][1]], axis=0).astype(BF16)

    lane = lax.broadcasted_iota(jnp.int32, (1, 128), 1)
    tok = lax.broadcasted_iota(jnp.int32, (toks, 1), 0)
    my_pos = jnp.where(tok < SPAN, place[2 * ctx], place[2 * ctx + 1]) * SPAN + (tok & (SPAN - 1))
    row = lax.broadcasted_iota(jnp.int32, (rows, 1), 0)
    limit = jnp.zeros((rows, 1), jnp.int32)
    for r in range(rows):
        limit = jnp.where(row == r, length[ctx * rows + r], limit)

    def scores(first, size, blocks, column):
        for j in range(size // 128):
            a, b = place[blocks[2 * j]], place[blocks[2 * j + 1]]
            pos = jnp.where(lane < SPAN, a, b) * SPAN + (lane & (SPAN - 1))
            cols = slice(j * 128, (j + 1) * 128)
            bias[:toks, cols] = jnp.where(pos <= my_pos, 0.0, MASKED)
            part = jnp.where(pos < limit, 0.0, MASKED)
            bias[toks:, cols] = jnp.concatenate([part] * (dec // rows), axis=0)
        from_keys = pl.ds(pl.multiple_of(first, 256), size)
        cols = pl.ds(pl.multiple_of(column, 256), size)
        half = pre // 2
        for begin, tall, extra in ((0, half, 0), (half, half, dec)):
            here = pl.ds(begin, tall + extra)
            add = [bias[:toks, :size]] * (tall // toks)
            if extra:
                add = add + [bias[toks:, :size]]
            s = dot(queries[here, :], keys[from_keys, :], 1, 1) + jnp.concatenate(add, axis=0)
            score[here, cols] = s
            best = top[here, :]
            for j in range(size // 128):
                best = jnp.maximum(best, s[:, j * 128 : (j + 1) * 128])
            top[here, :] = best

    def unit(dz, half, line):
        zz = at_z(dz)
        blocks = [2 * (j * NZ + zz) + half for j in range(NX)]
        scores(place_of(half, 0, zz), LINE, blocks, (line * 2 + half) * LINE)

    def full_line(dz, line):
        zz = at_z(dz)
        blocks = [2 * (j * NZ + zz) + half for half in (0, 1) for j in range(NX)]
        scores(place_of(0, 0, zz), 2 * LINE, blocks, line * 2 * LINE)

    def weigh(here, best, lines):
        den = jnp.zeros((best.shape[0], 128), F32)
        num = None
        for i, dz in enumerate(lines):
            e = jnp.exp2(score[here, i * 2 * LINE : (i + 1) * 2 * LINE] - best)
            for j in range(2 * LINE // 128):
                den = den + e[:, j * 128 : (j + 1) * 128]
            values = keys[pl.ds(pl.multiple_of(place_of(0, 0, at_z(dz)), 2 * LINE), 2 * LINE), :DL]
            part = dot(e.astype(BF16), values, 1, 0)
            num = part if num is None else num + part
        return num, den

    near, rest = (0, 1, -1), (3, -3, 4, 2, -2)

    def early(here, size):
        best = jnp.max(top[here, :], axis=1, keepdims=True)
        acc[here, :], part_den[here, :] = weigh(here, best, near)
        base[here, :] = jnp.broadcast_to(best, (size, 128))

    def join(here, best):
        num, den = weigh(here, best, rest)
        factor = jnp.exp2(base[here, :] - best)
        den = jnp.sum(den + part_den[here, :] * factor, axis=1, keepdims=True)
        return num + acc[here, :] * jnp.concatenate([factor] * (DL // 128), axis=1), den

    pl.loop(0, 2)(absorb)

    @on(0)
    def _():
        even_step(0)
        even_z(2)

    pl.loop(2, 4)(absorb)

    @on(0)
    def _():
        even_z(3)

    pl.loop(4, 6)(absorb)

    @on(0)
    def _():
        even_step(1)
        even_z(4)

    @on(1)
    def _():
        odd_line(0)

    @pl.when((core == 1) & (x != y))
    def _():
        odd_z(1)

    @on(1)
    def _():
        odd_z(2)

    pl.loop(6, heads // 2)(absorb)
    top[...] = jnp.full_like(top, MASKED)

    @on(0)
    def _():
        even_line(0)

    @on(1)
    def _():
        odd_z(3)

    @pl.loop(0, 2)
    def _(i):
        @pl.when((i == 1) & (core == 0))
        def _():
            even_step(2)

        @pl.when((i == 1) & (core == 1))
        def _():
            odd_z(4)

        @pl.when(i == 1)
        def _():
            twins_landed(0)

        unit(0, jnp.where(i == 0, core, 1 - core), 0)

    @on(0)
    def _():
        even_step(3)
        even_line(1)
        even_step(4)

    @on(1)
    def _():
        odd_step(1)
        odd_step(2)
        twins_landed(1)

    @pl.loop(0, 6)
    def _(i):
        @pl.when((i == 2) & (core == 0))
        def _():
            even_line(2)

        @pl.when((i == 4) & (core == 0))
        def _():
            even_line(3)
            twins_landed(1)

        @pl.when((i == 2) & (core == 1))
        def _():
            odd_line(1)
            odd_step(3)
            odd_step(4)

        @pl.when((i == 4) & (core == 1))
        def _():
            twins_landed(2)

        flip = lax.rem(i, 2)
        second = i // 2 == 2 - (1 - core)
        half = jnp.where((i < 2) | second, 0, 1)
        dz = jnp.where(second, 2, 1)
        unit(jnp.where(flip == 0, dz, -dz), half, jnp.where(second, 3, 1) + flip)

    @pl.loop(0, 4)
    def _(q):
        @pl.when((q == 1) & (core == 1))
        def _():
            odd_line(2)

        @pl.when((q == 3) & (core == 0))
        def _():
            even_line(4)

        @pl.when((q == 3) & (core == 1))
        def _():
            odd_line(3)

        early(pl.ds(pl.multiple_of(q * (pre // 4), 128), pre // 4), pre // 4)

    early(pl.ds(pre, dec), dec)

    @on(1)
    def _():
        odd_line(4)

    @on(0)
    def _():
        twins_landed(2)

    @pl.loop(0, 2)
    def _(i):
        unit(2 - 4 * i, 1, 3 + i)

    twins_landed(3)

    @pl.loop(0, 3)
    def _(i):
        @pl.when(i == 2)
        def _():
            twins_landed(NZ // 2)

        full_line(jnp.where(i == 2, NZ // 2, 3 - 6 * i), i)

    loads[2].wait()

    here = pl.ds(pre, dec)
    cache = dc_ref[...].astype(F32)
    own = jnp.concatenate([cache, cache[:, DL:]], axis=1)
    own = jnp.concatenate([own] * heads, axis=0)
    own_score = jnp.sum(queries[here, :].astype(F32) * own, axis=1, keepdims=True)
    best = jnp.maximum(jnp.max(top[here, :], axis=1, keepdims=True), own_score)
    num, den = join(here, best)
    own_weight = jnp.exp2(own_score - best)
    lat = (num + own_weight * own[:, :DL]) / (den + own_weight)
    high = lat.astype(BF16).astype(F32)
    low = lat - high
    outs = []
    for h in range(heads):
        part = slice(h * rows, (h + 1) * rows)
        pieces = jnp.concatenate([high[part], low[part]], axis=0).astype(BF16)
        doubled = dot(pieces, vup[:, h * DV : (h + 1) * DV], 1, 0)
        outs.append(doubled[:rows] + doubled[rows:])
    wide = heads // 2 * DV
    halves = [jnp.concatenate(outs[: heads // 2], axis=1), jnp.concatenate(outs[heads // 2 :], axis=1)]
    xrows[x] = jnp.concatenate(halves, axis=0).astype(BF16)

    def x_rows(d):
        return pltpu.make_async_remote_copy(
            src_ref=xrows.at[x], dst_ref=xrows.at[x], send_sem=dec_send.at[0],
            recv_sem=dec_recv.at[0], device_id=x_peer(d), device_id_type=MESH,
        )

    def z_rows(d):
        return pltpu.make_async_remote_copy(
            src_ref=zsend.at[at_z(d)], dst_ref=zrecv.at[d - 1], send_sem=dec_send.at[1],
            recv_sem=dec_recv.at[1], device_id=z_peer(d), device_id_type=MESH,
        )

    def whole(src, dst, send_sem, recv_sem):
        return pltpu.make_async_remote_copy(
            src_ref=src, dst_ref=dst, send_sem=send_sem, recv_sem=recv_sem,
            device_id=sibling, device_id_type=MESH,
        )

    all_x = whole(xrows.at[pl.ds(0, NX - 1)], xrows.at[pl.ds(0, NX - 1)], dec_send.at[0], dec_recv.at[0])
    all_z = whole(zsend.at[pl.ds(0, NZ - 1)], zrecv, dec_send.at[1], dec_recv.at[1])

    for d in range(1, NX):
        x_rows(d).start()

    share = out_ref.shape[0]
    width = heads * DV

    def deliver(first, size, d):
        other = lax.rem(member + d, 8)
        return pltpu.make_async_remote_copy(
            src_ref=staged.at[pl.ds(pl.multiple_of(other * share, share), share), pl.ds(first, size)],
            dst_ref=out_ref.at[:, pl.ds(pl.multiple_of(member * width + first, 128), size)],
            send_sem=out_send.at[0], recv_sem=out_recv.at[0],
            device_id=group_peer(d), device_id_type=MESH,
        )

    all_out = whole(
        staged.at[pl.ds(0, 7 * share), :], out_ref.at[:, pl.ds(0, 7 * width)],
        out_send.at[0], out_recv.at[0],
    )

    def sort_rows():
        all_x.wait_recv()
        tall = 2 * rows
        to = lax.broadcasted_iota(jnp.int32, (NZ * tall, NX * tall), 0)
        fro = lax.broadcasted_iota(jnp.int32, (NZ * tall, NX * tall), 1)
        target = (x * NZ + to // tall) * rows + (to & (rows - 1))
        slot = jnp.full((NZ * tall, NX * tall), -1, jnp.int32)
        for j in range(NX):
            for i in range(rows):
                hit = (fro // tall == j) & ((fro & (rows - 1)) == i)
                slot = jnp.where(hit, slots[(j * NZ + z) * rows + i], slot)
        pick = (slot == target) & ((to & rows) == (fro & rows))
        pick = jnp.where(pick, 1.0, 0.0).astype(BF16)
        moved = dot(pick, xrows[...].reshape(NX * tall, wide), 1, 0).astype(BF16)
        zsend[...] = moved.reshape(NZ, tall, wide)
        for d in range(1, NZ):
            z_rows(d).start()

    pairs = heads // 2
    cuts = (0, 3, 6, 7, 8)

    @pl.loop(0, pairs)
    def _(pair):
        here = pl.ds(pl.multiple_of(pair * 2 * toks, 2 * toks), 2 * toks)
        num, den = join(here, jnp.max(top[here, :], axis=1, keepdims=True))
        lat = (num * (1.0 / den)).astype(BF16)
        for sub in range(2):
            cols = pl.ds(pl.multiple_of((pair * 2 + sub) * DV, DV), DV)
            part = dot(lat[sub * toks : (sub + 1) * toks], vup[:, cols], 1, 0)
            staged[:, cols] = part.astype(BF16)
        pl.when(pair == 2)(sort_rows)
        for begin, end in zip(cuts[:-1], cuts[1:]):

            @pl.when(pair == end - 1)
            def _(begin=begin, end=end):
                for d in range(1, 8):
                    deliver(begin * 2 * DV, (end - begin) * 2 * DV, d).start()

    ours = pl.ds(pl.multiple_of(member * width, width), width)
    out_ref[:, ours] = staged[pl.ds(pl.multiple_of(member * share, share), share), :]
    all_z.wait_recv()
    total = zsend[z].astype(F32)
    for d in range(1, NZ):
        total = total + zrecv[d - 1].astype(F32)
    dec_ref[...] = jnp.concatenate([total[:rows], total[rows:]], axis=1).astype(BF16)
    sent = 2 * NX * NZ * SPAN - SPAN

    whole(keys.at[pl.ds(0, sent), :], keys.at[pl.ds(0, sent), :], send.at[0], recv.at[0]).wait_send()
    all_x.wait_send()
    all_z.wait_send()
    all_out.wait_send()
    all_out.wait_recv()


def hand_on(a, b, to_a, to_b, sems):
    copies = [pltpu.make_async_copy(a, to_a, sems.at[0]), pltpu.make_async_copy(b, to_b, sems.at[1])]
    for one in copies:
        one.start()
    for one in copies:
        one.wait()


def per_device(
    prefill_query, prompt_cache, key_up, value_up, block_place, decode_query, decode_cache,
    row_length, row_slot,
):
    toks, width = prefill_query.shape
    heads = width // HD
    rows = decode_query.shape[0]
    count = NX * NZ * toks
    smem = pl.BlockSpec(memory_space=pltpu.SMEM)
    vmem = pl.BlockSpec(memory_space=pltpu.VMEM)
    hbm = pl.BlockSpec(memory_space=pl.ANY)
    total = heads * (toks + rows)
    wide = heads // 2 * DV
    moved = pl.pallas_call(
        kernel,
        out_shape=(
            jax.ShapeDtypeStruct((toks // 8, 8 * heads * DV), BF16),
            jax.ShapeDtypeStruct((rows, heads * DV), BF16),
        ),
        in_specs=[smem, smem, smem, vmem, vmem, vmem, hbm, hbm, hbm],
        out_specs=(vmem, vmem),
        scratch_shapes=[
            pltpu.VMEM((toks, width), BF16),
            pltpu.VMEM((count, WIDE), BF16),
            pltpu.VMEM(key_up.shape, BF16),
            pltpu.VMEM(value_up.shape, BF16),
            pltpu.VMEM((total, WIDE), BF16),
            pltpu.VMEM((total, 5 * 2 * LINE), F32),
            pltpu.VMEM((total, 128), F32),
            pltpu.VMEM((total, DL), F32),
            pltpu.VMEM((total, 128), F32),
            pltpu.VMEM((total, 128), F32),
            pltpu.VMEM((toks + heads * rows, 2 * LINE), F32),
            pltpu.VMEM((toks, heads * DV), BF16),
            pltpu.VMEM((NX, 2 * rows, wide), BF16),
            pltpu.VMEM((NZ, 2 * rows, wide), BF16),
            pltpu.VMEM((NZ - 1, 2 * rows, wide), BF16),
            pltpu.SemaphoreType.DMA((3,)),
            pltpu.SemaphoreType.DMA((1,)),
            pltpu.SemaphoreType.DMA((26,)),
            pltpu.SemaphoreType.DMA((1,)),
            pltpu.SemaphoreType.DMA((1,)),
            pltpu.SemaphoreType.DMA((2,)),
            pltpu.SemaphoreType.DMA((2,)),
        ],
        compiler_params=pltpu.CompilerParams(
            vmem_limit_bytes=60 << 20, collective_id=0, has_side_effects=True
        ),
    )(
        block_place, row_length, row_slot, prompt_cache.T, decode_query, decode_cache,
        prefill_query, key_up, value_up,
    )
    return pl.pallas_call(
        hand_on,
        out_shape=tuple(jax.ShapeDtypeStruct(one.shape, one.dtype) for one in moved),
        in_specs=[vmem, vmem],
        out_specs=(hbm, hbm),
        scratch_shapes=[pltpu.SemaphoreType.DMA((2,))],
    )(*moved)


def solution(mesh):
    return jax.shard_map(
        per_device,
        mesh=mesh,
        in_specs=(
            P("ctx", ("tp", "grp")),
            P("ctx", None),
            P(None, ("tp", "grp")),
            P(None, ("tp", "grp")),
            P(),
            P("ctx", ("tp", "grp")),
            P("ctx", None),
            P(),
            P(),
        ),
        out_specs=(P(("ctx", "tp", "grp"), None), P("ctx", ("tp", "grp"))),
        check_vma=False,
    )
```

profile of v0, /device:TPU:1, one launch (start us, length us, event | category | flops | bytes accessed | tf_op | source)
XLA Modules:
  0.0 65.7 jit_solution(12456749275642034275)
XLA Ops:
  0.6 63.2 %shard_map.104 = (bf16[16,16384]{1,0:T(8,128)(2,1)}, bf16[8,2048]{1,0:T(8,128)(2,1)}) custom-call(s32[64]{0:T(128)} %place.1, s32[256]{0:T(256)} %length.1, s32[256]{0:T(256)} %slots.1, bf16[576,128]{1,0:T(8,128)(2,1)} %bitcast.1, bf16[8,3072]{1,0:T(8,128)(2,1)} %dq_ref.1, bf16[8,576]{1,0:T(8,128)(2,1)} %dc_ref.1, bf16[128,3072]{1,0:T(8,128)(2,1)} %q_hbm.1, ...), custom_call_target="tpu_custom_call" | custom-call | tf_op jit(solution)/shard_map/pallas_call | solution.py:532
  63.8 1.9 %shard_map.105 = (bf16[16,16384]{1,0:T(8,128)(2,1)}, bf16[8,2048]{1,0:T(8,128)(2,1)}) custom-call(bf16[16,16384]{1,0:T(8,128)(2,1)} %get-tuple-element.4.a, bf16[8,2048]{1,0:T(8,128)(2,1)} %get-tuple-element.5.b), custom_call_target="tpu_custom_call" | custom-call | tf_op jit(solution)/shard_map/pallas_call | solution.py:571
where the time goes:
time: 65.8 us; the launch traced here: 65.7 us
  Pallas kernels  65 us (99%)
    pallas_call x1, Pallas kernels, per_device(): pl.pallas_call(kernel, out_shape=(jax.ShapeDtypeStruct((toks // 8, 8 * he...  63.2 us
    pallas_call x1, Pallas kernels, per_device(): pl.pallas_call(hand_on, out_shape=tuple((jax.ShapeDtypeStruct(one.shape,...  1.86 us

commit v1 on v0

--- a/solution.py
+++ b/solution.py
@@ -111,7 +111,7 @@
     def on(which):
         return pl.when(core == which)
 
-    EVEN_Z, ODD_Z, TWIN, EVEN_X, ODD_Y, ODD_X = 0, 5, 10, 15, 20, 25
+    EVEN_Z, ODD_Z, TWIN, EVEN_X, ODD_Y, ODD_X = 0, 8, 16, 24, 32, 40
     far = NZ // 2
 
     def signs(k):
@@ -119,36 +119,38 @@
 
     def even_z(k):
         first = place_of(0, x, z)
-        start([copy(first, SPAN, EVEN_Z + k, z_peer(dz)) for dz in signs(k)])
+        start([copy(first, SPAN, EVEN_Z + (-d) % NZ, z_peer(d)) for d in signs(k)])
 
     def odd_z(k):
         first = place_of(1, y, z)
-        start([copy(first, SPAN, ODD_Z + k, z_peer(dz)) for dz in signs(k)])
+        start([copy(first, SPAN, ODD_Z + (-d) % NZ, z_peer(d)) for d in signs(k)])
 
     def even_step(k):
-        if k:
-            landed(EVEN_Z + k, SPAN * len(signs(k)))
         for dz in signs(k):
-            start([copy(place_of(0, x, at_z(dz)), SPAN, EVEN_X + k, x_peer(d)) for d in (1, 3, 2)])
+            if k:
+                landed(EVEN_Z + dz % NZ, SPAN)
+            first = place_of(0, x, at_z(dz))
+            start([copy(first, SPAN, EVEN_X + dz % NZ, x_peer(d)) for d in (1, 3, 2)])
 
     def odd_step(k):
-        landed(ODD_Z + k, SPAN * len(signs(k)))
         for dz in signs(k):
-            start([copy(place_of(1, y, at_z(dz)), SPAN, ODD_Y + k, y_peer(d)) for d in (1, 3, 2)])
+            landed(ODD_Z + dz % NZ, SPAN)
+            first = place_of(1, y, at_z(dz))
+            start([copy(first, SPAN, ODD_Y + dz % NZ, y_peer(d)) for d in (1, 3, 2)])
 
     def twin(dz):
-        return copy(place_of(core, 0, at_z(dz)), LINE, TWIN + abs(dz), sibling)
-
-    def even_line(k):
-        landed(EVEN_X + k, 3 * SPAN * len(signs(k)))
-        start([twin(dz) for dz in signs(k)])
-
-    def odd_line(k):
-        landed(ODD_Y + k if k else ODD_X, 3 * SPAN * len(signs(k)))
-        start([twin(dz) for dz in signs(k)])
-
-    def twins_landed(k):
-        landed(TWIN + k, LINE * len(signs(k)))
+        return copy(place_of(core, 0, at_z(dz)), LINE, TWIN + dz % NZ, sibling)
+
+    def even_line(dz):
+        landed(EVEN_X + dz % NZ, 3 * SPAN)
+        twin(dz).start()
+
+    def odd_line(dz):
+        landed(ODD_Y + dz % NZ if dz else ODD_X, 3 * SPAN)
+        twin(dz).start()
+
+    def twin_landed(dz):
+        landed(TWIN + dz % NZ, LINE)
 
     @on(0)
     def _():
@@ -307,7 +309,7 @@
 
         @pl.when(i == 1)
         def _():
-            twins_landed(0)
+            twin_landed(0)
 
         unit(0, jnp.where(i == 0, core, 1 - core), 0)
 
@@ -321,28 +323,54 @@
     def _():
         odd_step(1)
         odd_step(2)
-        twins_landed(1)
+        twin_landed(1)
 
     @pl.loop(0, 6)
     def _(i):
-        @pl.when((i == 2) & (core == 0))
+        def at(turn, which):
+            return pl.when((i == turn) & (core == which))
+
+        @at(1, 0)
+        def _():
+            even_line(-1)
+
+        @at(1, 1)
+        def _():
+            twin_landed(-1)
+
+        @at(2, 0)
         def _():
             even_line(2)
 
-        @pl.when((i == 4) & (core == 0))
-        def _():
-            even_line(3)
-            twins_landed(1)
-
-        @pl.when((i == 2) & (core == 1))
+        @at(2, 1)
         def _():
             odd_line(1)
             odd_step(3)
+
+        @at(3, 0)
+        def _():
+            even_line(-2)
+
+        @at(3, 1)
+        def _():
+            odd_line(-1)
             odd_step(4)
 
-        @pl.when((i == 4) & (core == 1))
-        def _():
-            twins_landed(2)
+        @at(4, 0)
+        def _():
+            twin_landed(1)
+
+        @at(4, 1)
+        def _():
+            twin_landed(2)
+
+        @at(5, 0)
+        def _():
+            twin_landed(-1)
+
+        @at(5, 1)
+        def _():
+            twin_landed(-2)
 
         flip = lax.rem(i, 2)
         second = i // 2 == 2 - (1 - core)
@@ -352,17 +380,24 @@
 
     @pl.loop(0, 4)
     def _(q):
+        @pl.when((q == 1) & (core == 0))
+        def _():
+            even_line(3)
+            even_line(-3)
+
         @pl.when((q == 1) & (core == 1))
         def _():
             odd_line(2)
+            odd_line(-2)
 
         @pl.when((q == 3) & (core == 0))
         def _():
-            even_line(4)
+            even_line(far)
 
         @pl.when((q == 3) & (core == 1))
         def _():
             odd_line(3)
+            odd_line(-3)
 
         early(pl.ds(pl.multiple_of(q * (pre // 4), 128), pre // 4), pre // 4)
 
@@ -370,23 +405,25 @@
 
     @on(1)
     def _():
-        odd_line(4)
+        odd_line(far)
 
     @on(0)
     def _():
-        twins_landed(2)
+        twin_landed(2)
+        twin_landed(-2)
 
     @pl.loop(0, 2)
     def _(i):
         unit(2 - 4 * i, 1, 3 + i)
 
-    twins_landed(3)
+    twin_landed(3)
+    twin_landed(-3)
 
     @pl.loop(0, 3)
     def _(i):
         @pl.when(i == 2)
         def _():
-            twins_landed(NZ // 2)
+            twin_landed(far)
 
         full_line(jnp.where(i == 2, NZ // 2, 3 - 6 * i), i)
 
@@ -555,7 +592,7 @@
             pltpu.VMEM((NZ - 1, 2 * rows, wide), BF16),
             pltpu.SemaphoreType.DMA((3,)),
             pltpu.SemaphoreType.DMA((1,)),
-            pltpu.SemaphoreType.DMA((26,)),
+            pltpu.SemaphoreType.DMA((41,)),
             pltpu.SemaphoreType.DMA((1,)),
             pltpu.SemaphoreType.DMA((1,)),
             pltpu.SemaphoreType.DMA((2,)),

time: 65.8 us -> 65.5 us (level)
  no operation moved by 1% of the time
where the time goes in v1:
time: 65.5 us; the launch traced here: 65.3 us
  Pallas kernels  64.7 us (99%)
    pallas_call x1, Pallas kernels, per_device(): pl.pallas_call(kernel, out_shape=(jax.ShapeDtypeStruct((toks // 8, 8 * he...  62.8 us
    pallas_call x1, Pallas kernels, per_device(): pl.pallas_call(hand_on, out_shape=tuple((jax.ShapeDtypeStruct(one.shape,...  1.86 us

profile of v1, /device:TPU:1, one launch (start us, length us, event | category | flops | bytes accessed | tf_op | source)
XLA Modules:
  0.0 65.3 jit_solution(13490955761077072382)
XLA Ops:
  0.6 62.8 %shard_map.104 = (bf16[16,16384]{1,0:T(8,128)(2,1)}, bf16[8,2048]{1,0:T(8,128)(2,1)}) custom-call(s32[64]{0:T(128)} %place.1, s32[256]{0:T(256)} %length.1, s32[256]{0:T(256)} %slots.1, bf16[576,128]{1,0:T(8,128)(2,1)} %bitcast.1, bf16[8,3072]{1,0:T(8,128)(2,1)} %dq_ref.1, bf16[8,576]{1,0:T(8,128)(2,1)} %dc_ref.1, bf16[128,3072]{1,0:T(8,128)(2,1)} %q_hbm.1, ...), custom_call_target="tpu_custom_call" | custom-call | tf_op jit(solution)/shard_map/pallas_call | solution.py:569
  63.5 1.9 %shard_map.105 = (bf16[16,16384]{1,0:T(8,128)(2,1)}, bf16[8,2048]{1,0:T(8,128)(2,1)}) custom-call(bf16[16,16384]{1,0:T(8,128)(2,1)} %get-tuple-element.4.a, bf16[8,2048]{1,0:T(8,128)(2,1)} %get-tuple-element.5.b), custom_call_target="tpu_custom_call" | custom-call | tf_op jit(solution)/shard_map/pallas_call | solution.py:608

commit v2 on v1

--- a/solution.py
+++ b/solution.py
@@ -521,12 +521,12 @@
             cols = pl.ds(pl.multiple_of((pair * 2 + sub) * DV, DV), DV)
             part = dot(lat[sub * toks : (sub + 1) * toks], vup[:, cols], 1, 0)
             staged[:, cols] = part.astype(BF16)
-        pl.when(pair == 2)(sort_rows)
+        pl.when(pair == 3)(sort_rows)
         for begin, end in zip(cuts[:-1], cuts[1:]):
 
             @pl.when(pair == end - 1)
             def _(begin=begin, end=end):
-                for d in range(1, 8):
+                for d in (4, 2, 6, 3, 5, 1, 7):
                     deliver(begin * 2 * DV, (end - begin) * 2 * DV, d).start()
 
     ours = pl.ds(pl.multiple_of(member * width, width), width)

time: 65.5 us -> 64.9 us (level)
  no operation moved by 1% of the time
where the time goes in v2:
time: 64.9 us; the launch traced here: 64.8 us
  Pallas kernels  64.2 us (99%)
    pallas_call x1, Pallas kernels, per_device(): pl.pallas_call(kernel, out_shape=(jax.ShapeDtypeStruct((toks // 8, 8 * he...  62.3 us
    pallas_call x1, Pallas kernels, per_device(): pl.pallas_call(hand_on, out_shape=tuple((jax.ShapeDtypeStruct(one.shape,...  1.86 us

profile of v2, /device:TPU:1, one launch (start us, length us, event | category | flops | bytes accessed | tf_op | source)
XLA Modules:
  0.0 64.8 jit_solution(16643012154041766314)
XLA Ops:
  0.6 62.3 %shard_map.104 = (bf16[16,16384]{1,0:T(8,128)(2,1)}, bf16[8,2048]{1,0:T(8,128)(2,1)}) custom-call(s32[64]{0:T(128)} %place.1, s32[256]{0:T(256)} %length.1, s32[256]{0:T(256)} %slots.1, bf16[576,128]{1,0:T(8,128)(2,1)} %bitcast.1, bf16[8,3072]{1,0:T(8,128)(2,1)} %dq_ref.1, bf16[8,576]{1,0:T(8,128)(2,1)} %dc_ref.1, bf16[128,3072]{1,0:T(8,128)(2,1)} %q_hbm.1, ...), custom_call_target="tpu_custom_call" | custom-call | tf_op jit(solution)/shard_map/pallas_call | solution.py:569
  63.0 1.9 %shard_map.105 = (bf16[16,16384]{1,0:T(8,128)(2,1)}, bf16[8,2048]{1,0:T(8,128)(2,1)}) custom-call(bf16[16,16384]{1,0:T(8,128)(2,1)} %get-tuple-element.4.a, bf16[8,2048]{1,0:T(8,128)(2,1)} %get-tuple-element.5.b), custom_call_target="tpu_custom_call" | custom-call | tf_op jit(solution)/shard_map/pallas_call | solution.py:608

commit v3 on v2

--- a/solution.py
+++ b/solution.py
@@ -155,6 +155,7 @@
     @on(0)
     def _():
         even_z(1)
+        even_step(0)
 
     @on(1)
     def _():
@@ -258,7 +259,6 @@
 
     @on(0)
     def _():
-        even_step(0)
         even_z(2)
 
     pl.loop(2, 4)(absorb)

time: 64.9 us -> 64.5 us (level)
  no operation moved by 1% of the time
where the time goes in v3:
time: 64.5 us; the launch traced here: 64.4 us
  Pallas kernels  63.8 us (99%)
    pallas_call x1, Pallas kernels, per_device(): pl.pallas_call(kernel, out_shape=(jax.ShapeDtypeStruct((toks // 8, 8 * he...  61.9 us
    pallas_call x1, Pallas kernels, per_device(): pl.pallas_call(hand_on, out_shape=tuple((jax.ShapeDtypeStruct(one.shape,...  1.86 us

profile of v3, /device:TPU:1, one launch (start us, length us, event | category | flops | bytes accessed | tf_op | source)
XLA Modules:
  0.0 64.4 jit_solution(12055859214514428890)
XLA Ops:
  0.6 61.9 %shard_map.104 = (bf16[16,16384]{1,0:T(8,128)(2,1)}, bf16[8,2048]{1,0:T(8,128)(2,1)}) custom-call(s32[64]{0:T(128)} %place.1, s32[256]{0:T(256)} %length.1, s32[256]{0:T(256)} %slots.1, bf16[576,128]{1,0:T(8,128)(2,1)} %bitcast.1, bf16[8,3072]{1,0:T(8,128)(2,1)} %dq_ref.1, bf16[8,576]{1,0:T(8,128)(2,1)} %dc_ref.1, bf16[128,3072]{1,0:T(8,128)(2,1)} %q_hbm.1, ...), custom_call_target="tpu_custom_call" | custom-call | tf_op jit(solution)/shard_map/pallas_call | solution.py:569
  62.6 1.9 %shard_map.105 = (bf16[16,16384]{1,0:T(8,128)(2,1)}, bf16[8,2048]{1,0:T(8,128)(2,1)}) custom-call(bf16[16,16384]{1,0:T(8,128)(2,1)} %get-tuple-element.4.a, bf16[8,2048]{1,0:T(8,128)(2,1)} %get-tuple-element.5.b), custom_call_target="tpu_custom_call" | custom-call | tf_op jit(solution)/shard_map/pallas_call | solution.py:608
